TPU v7x, 128 devices: a whole 4x4x4 slice. The times are simulated.
128 devices in a mesh: slot: 4 (over y), region: 32 (over z, x, core).
Axes of the slice: x: 4, y: 4, z: 4, core: 2. Of those that a mesh axis runs over, the one named last changes fastest.
Arguments:
- residual: float32 [4, 2, 685, 16384], P('slot', None, None, 'region'), may hold values from -32 to 32
- perturb: bfloat16 [4, 64, 685, 4096], P('slot', None, None, 'region'), may hold values from -3 to 3
- vertical_modes: float32 [685, 10], replicated, may hold values from -0.21875 to 0.21875
- column_weight: float32 [16384], P('region'), may hold values from 0.5 to 1.5
- owner_table: int32 [16384, 1], replicated, may hold values from 0 to 31; in each aligned block of 512 rows (0 to 511, 512 to 1023, ...) at most 32 rows name the same one
- column_map: int32 [16384], replicated, may hold values from 0 to 127
Outputs:
- hess_product: float32 [4, 2, 685, 16384], P('slot', None, None, 'region')
- step_length: float32 [2], replicated
- next_residual: float32 [4, 2, 685, 16384], P('slot', None, None, 'region')
Inputs may be any that keep to these rules, and one draw needn't show every extreme that they name: `owner_table`: among the 512 fine columns of one region, at most 32 name the same owner, a bound that some block reaches.
All inputs are finite; a program needn't handle non-finite values.
Results may differ from a plain program's by a relative error of at most 0.004.
Values may be sent and summed in bfloat16 or wider, within the bound.
A program may use at most 128 MiB of HBM per device.

v0:
```python
import jax
import jax.numpy as jnp
from jax import lax
from jax.experimental import pallas as pl
from jax.experimental.pallas import tpu as pltpu
from jax.sharding import PartitionSpec as P

MESH = pl.DeviceIdType.MESH
LAT_ROWS = 8
DIFFUSION_RATE = 0.2
F32 = jnp.float32
BF16 = jnp.bfloat16

REGIONS = 32
CAP = 32
SLOTS = 4
FINE = 512
COARSE = 128
FEAT = 685
FEAT_PAD = 688
WIDE = 1408
MEMBERS = 64
MODES = 10
ROWS = MODES * MEMBERS
SHARE = ROWS // SLOTS
OUT_CUT = 768
BACK_CUT = 640

NEAR_FIRST = (
    [(0, 1), (1, 0), (0, 3), (3, 0)],
    [(1, 1), (3, 3), (1, 3), (3, 1)],
    [(2, 0), (0, 2)],
    [(2, 1), (1, 2), (2, 3), (3, 2)],
    [(2, 2)],
)
HOPS = [(z, x, c) for group in NEAR_FIRST[::-1] for c in (0, 1) for z, x in group] + [(0, 0, 1)]


def smooth(cells, west_from, east_from):
    lane = lax.broadcasted_iota(jnp.int32, cells.shape, 1)
    row = lane % LAT_ROWS
    west = pltpu.roll(jnp.where(lane >= COARSE - LAT_ROWS, west_from, cells), LAT_ROWS, 1)
    east = pltpu.roll(jnp.where(lane < LAT_ROWS, east_from, cells), COARSE - LAT_ROWS, 1)
    south = pltpu.roll(cells, 1, 1)
    north = pltpu.roll(cells, COARSE - 1, 1)
    along = jnp.where(row > 0, south - cells, 0.0) + jnp.where(row < LAT_ROWS - 1, north - cells, 0.0)
    return cells + DIFFUSION_RATE * (west + east - 2.0 * cells + along)


def dot(a, b):
    return jnp.dot(a, b, preferred_element_type=F32)


def kernel(
    owners_ref,
    map_ref,
    weight_ref,
    modes_t_ref,
    modes_b_ref,
    resid_hbm,
    members_hbm,
    fine_ref,
    step_ref,
    resid,
    members,
    wide_rows,
    wide_cols,
    slot_hot_t,
    slot_hot,
    place,
    place_t,
    send_a,
    send_b,
    recv_a,
    recv_b,
    coarse,
    control,
    summed_in,
    edge_out,
    edge_in,
    shares,
    gathered,
    smoothed,
    total,
    total_t,
    back_a,
    back_b,
    home_a,
    home_b,
    norm,
    norm_in,
    norm_sum,
    norm_all,
    load_sem,
    out_send,
    out_recv,
    back_send,
    back_recv,
    sum_send,
    sum_recv,
    edge_send,
    edge_recv,
    share_send,
    share_recv,
    norm_send,
    norm_recv,
    last_send,
    last_recv,
):
    me = lax.axis_index("region")
    slot = lax.axis_index("slot")
    z, x, core = me // 8, (me // 2) % 4, me % 2

    def region_at(hop):
        dz, dx, dc = hop
        return (((z + dz) % 4) * 4 + (x + dx) % 4) * 2 + (core + dc) % 2

    partners = [region_at(h) for h in HOPS]
    load_resid = pltpu.make_async_copy(resid_hbm, resid, load_sem.at[0])
    load_resid.start()
    load_members = pltpu.make_async_copy(members_hbm, members, load_sem.at[1])
    load_members.start()

    barrier = pltpu.get_barrier_semaphore()
    for p in partners:
        pl.semaphore_signal(barrier, inc=1, device_id={"region": p}, device_id_type=MESH)
    for d in (1, 2, 3):
        pl.semaphore_signal(barrier, inc=1, device_id={"slot": (slot + d) % SLOTS}, device_id_type=MESH)

    own = owners_ref[pl.ds(me, 1), :]
    owner_hot = (lax.broadcasted_iota(jnp.int32, (REGIONS, FINE), 0) == own).astype(BF16)
    earlier = (
        lax.broadcasted_iota(jnp.int32, (FINE, FINE), 0) < lax.broadcasted_iota(jnp.int32, (FINE, FINE), 1)
    ).astype(BF16)
    before = dot(owner_hot, earlier)
    rank = jnp.sum(owner_hot.astype(F32) * before, axis=0, keepdims=True)
    my_slots = own * CAP + rank.astype(jnp.int32)
    for q in range(4):
        rows = pl.ds(q * 256, 256)
        hot = lax.broadcasted_iota(jnp.int32, (256, FINE), 0) + q * 256 == my_slots
        slot_hot_t[rows, :] = hot.astype(F32).astype(BF16)

    wide_rows[pl.ds(1373, WIDE - 1373), :] = jnp.zeros((WIDE - 1373, FINE), F32)
    index_row = (map_ref[pl.ds(me, 1), :] + 1).astype(F32)
    wide_rows[pl.ds(FEAT, 3), :] = jnp.broadcast_to(index_row, (3, FINE))
    load_resid.wait()
    norm[...] = jnp.zeros_like(norm)
    for v in range(2):
        field = resid[v]
        wide_rows[pl.ds(v * FEAT_PAD, FEAT), :] = field * weight_ref[...]
        by_col = jnp.sum(field * field, axis=0, keepdims=True)
        norm[pl.ds(v, 1), :] = by_col[:, 0:128] + by_col[:, 128:256] + by_col[:, 256:384] + by_col[:, 384:512]
    for q in range(4):
        wide_cols[pl.ds(q * 128, 128), :] = wide_rows[:, q * 128 : (q + 1) * 128].T.astype(BF16)

    pl.semaphore_wait(barrier, len(HOPS) + 3)

    def pack(out, left, matrix, depth_rows, width):
        def one(q, carry):
            got = dot(matrix[pl.ds(pl.multiple_of(q * 256, 256), 256), :], depth_rows[:, left : left + width])
            out[pl.ds(q * 8, 8)] = got.astype(BF16).reshape(8, CAP, width)
            return carry

        lax.fori_loop(0, 4, one, 0)

    def exchange(source, landing, chunk, send_sems, recv_sems):
        copies = []
        for i, p in enumerate(partners):
            copy = pltpu.make_async_remote_copy(
                src_ref=source.at[p],
                dst_ref=landing.at[me],
                send_sem=send_sems.at[chunk, i],
                recv_sem=recv_sems.at[chunk, i],
                device_id={"region": p},
                device_id_type=MESH,
            )
            copy.start()
            copies.append(copy)
        landing[me] = source[me]
        return copies

    pack(send_a, 0, slot_hot_t, wide_cols, OUT_CUT)
    out_copies = exchange(send_a, recv_a, 0, out_send, out_recv)
    pack(send_b, OUT_CUT, slot_hot_t, wide_cols, WIDE - OUT_CUT)
    out_copies_b = exchange(send_b, recv_b, 1, out_send, out_recv)

    slot_hot[...] = slot_hot_t[...].T
    total[...] = jnp.zeros_like(total)
    smoothed[...] = jnp.zeros_like(smoothed)
    load_members.wait()

    def contract(v):
        field = coarse[pl.ds(v * FEAT_PAD, FEAT), :]

        def pair(i, carry):
            halves = [(members[2 * i + e].astype(F32) * field).astype(BF16) for e in range(2)]
            got = dot(modes_t_ref[...], jnp.concatenate(halves, axis=1))
            got = got[0:16] + got[16:32]
            for e in range(2):
                control[pl.ds(v * ROWS + 2 * i + e, MODES, stride=MEMBERS), :] = got[
                    0:MODES, e * COARSE : (e + 1) * COARSE
                ]
            return carry

        lax.fori_loop(0, MEMBERS // 2, pair, 0)

    def share_rows(v, t):
        return pl.ds(pl.multiple_of(v * ROWS + t * SHARE, 8), SHARE)

    def sum_start(v):
        copies = []
        for d in (2, 1, 3):
            t = (slot + d) % SLOTS
            copy = pltpu.make_async_remote_copy(
                src_ref=control.at[share_rows(v, t)],
                dst_ref=summed_in.at[v, d - 1],
                send_sem=sum_send.at[v, d - 1],
                recv_sem=sum_recv.at[v, d - 1],
                device_id={"slot": t},
                device_id_type=MESH,
            )
            copy.start()
            copies.append(copy)
        return copies

    def edges_start(v):
        cells = control[share_rows(v, slot), :]
        for d in range(3):
            cells = cells + summed_in[v, d]
        shares[v] = cells
        lane = lax.broadcasted_iota(jnp.int32, (40, COARSE), 1)
        east = jnp.zeros((40, COARSE), F32)
        west = jnp.zeros((40, COARSE), F32)
        for g in range(4):
            part = cells[g * 40 : (g + 1) * 40]
            mine = lane // 16 == g
            east = jnp.where(mine, pltpu.roll(part, 16 * g + 16, 1), east)
            west = jnp.where(mine, pltpu.roll(part, 16 * g, 1) if g else part, west)
        edge_out[v, 0] = east
        edge_out[v, 1] = west
        copies = []
        for side, p in ((0, (me + 1) % REGIONS), (1, (me + REGIONS - 1) % REGIONS)):
            copy = pltpu.make_async_remote_copy(
                src_ref=edge_out.at[v, side],
                dst_ref=edge_in.at[v, side],
                send_sem=edge_send.at[v, side],
                recv_sem=edge_recv.at[v, side],
                device_id={"region": p},
                device_id_type=MESH,
            )
            copy.start()
            copies.append(copy)
        return copies

    def smooth_share(v):
        cells = shares[v]
        lane = lax.broadcasted_iota(jnp.int32, (SHARE, COARSE), 1)
        west = jnp.concatenate([pltpu.roll(edge_in[v, 0], 112 - 16 * g, 1) for g in range(4)], axis=0)
        east = jnp.concatenate(
            [pltpu.roll(edge_in[v, 1], 128 - 16 * g, 1) if g else edge_in[v, 1] for g in range(4)], axis=0
        )
        once = smooth(cells, west, east)
        west = jnp.where(lane < LAT_ROWS, cells, west)
        east = jnp.where(lane >= COARSE - LAT_ROWS, cells, east)
        twice = smooth(once, smooth(west, west, west), smooth(east, east, east))
        norm[pl.ds(2 + v, 1), :] = jnp.sum(once * once, axis=0, keepdims=True)
        smooth_bits = twice.astype(BF16)
        gathered[v, slot] = smooth_bits
        copies = []
        for d in (2, 1, 3):
            copy = pltpu.make_async_remote_copy(
                src_ref=gathered.at[v, slot],
                dst_ref=gathered.at[v, slot],
                send_sem=share_send.at[v, d - 1],
                recv_sem=share_recv.at[v, d - 1],
                device_id={"slot": (slot + d) % SLOTS},
                device_id_type=MESH,
            )
            copy.start()
            copies.append(copy)
        return copies

    def expand(v):
        for t in range(SLOTS):
            smoothed[pl.ds(t * SHARE, SHARE), :] = gathered[v, t].astype(F32)

        def pair(i, carry):
            halves = []
            for e in range(2):
                cells = smoothed[pl.ds(2 * i + e, 16, stride=MEMBERS), :].astype(BF16)
                halves.append(jnp.concatenate([cells, cells], axis=0))
            mixed = dot(modes_b_ref[...], jnp.concatenate(halves, axis=1))
            total[pl.ds(v * FEAT_PAD, FEAT), :] += (
                members[2 * i].astype(F32) * mixed[:, 0:COARSE]
                + members[2 * i + 1].astype(F32) * mixed[:, COARSE : 2 * COARSE]
            )
            return carry

        lax.fori_loop(0, MEMBERS // 2, pair, 0)


    def arrived(copies):
        for copy in copies:
            copy.wait_recv()

    def back_start(chunk):
        left, width = ((0, BACK_CUT), (BACK_CUT, WIDE - BACK_CUT))[chunk]
        out = (back_a, back_b)[chunk]
        total_t[:, left : left + width] = total[pl.ds(left, width), :].T.astype(BF16)
        pack(out, left, place, total_t, width)
        return exchange(out, (home_a, home_b)[chunk], chunk, back_send, back_recv)

    def fine_rows(chunk):
        left, width = ((0, BACK_CUT), (BACK_CUT, WIDE - BACK_CUT))[chunk]
        home = (home_a, home_b)[chunk][...].reshape(REGIONS * CAP, width)
        for q in range(4):
            got = dot(slot_hot[pl.ds(q * 128, 128), :], home)
            fine_ref[pl.ds(left, width), q * 128 : (q + 1) * 128] = got.T.astype(BF16)

    arrived(out_copies)
    sent = recv_a[...].reshape(REGIONS * CAP, OUT_CUT)
    near = sent[:, 640:768].astype(F32)
    lane = lax.broadcasted_iota(jnp.int32, (REGIONS * CAP, COARSE), 1)
    index = jnp.sum(jnp.where(lane == FEAT - 640, near, 0.0), axis=1, keepdims=True)
    hot = (lane + 1).astype(F32) == index
    place[...] = hot.astype(F32).astype(BF16)
    place_t[...] = place[...].T
    coarse[pl.ds(0, OUT_CUT), :] = dot(place_t[...], sent).T
    contract(0)
    sum_copies = sum_start(0)
    arrived(sum_copies)
    edge_copies = edges_start(0)
    arrived(edge_copies)
    share_copies = smooth_share(0)

    arrived(out_copies_b)
    coarse[pl.ds(OUT_CUT, WIDE - OUT_CUT), :] = dot(
        place_t[...], recv_b[...].reshape(REGIONS * CAP, WIDE - OUT_CUT)
    ).T
    contract(1)
    sum_copies_b = sum_start(1)

    arrived(share_copies)
    expand(0)
    back_copies = back_start(0)

    arrived(sum_copies_b)
    edge_copies_b = edges_start(1)
    arrived(edge_copies_b)
    share_copies_b = smooth_share(1)
    norm_copies = []
    for d in (2, 1, 3):
        copy = pltpu.make_async_remote_copy(
            src_ref=norm,
            dst_ref=norm_in.at[d - 1],
            send_sem=norm_send.at[d - 1],
            recv_sem=norm_recv.at[d - 1],
            device_id={"slot": (slot + d) % SLOTS},
            device_id_type=MESH,
        )
        copy.start()
        norm_copies.append(copy)
    arrived(share_copies_b)
    expand(1)
    back_copies_b = back_start(1)
    arrived(norm_copies)
    norm_sum[...] = norm[...] + norm_in[0] + norm_in[1] + norm_in[2]
    last_copies = []
    for i, p in enumerate(partners):
        copy = pltpu.make_async_remote_copy(
            src_ref=norm_sum,
            dst_ref=norm_all.at[me],
            send_sem=last_send.at[i],
            recv_sem=last_recv.at[i],
            device_id={"region": p},
            device_id_type=MESH,
        )
        copy.start()
        last_copies.append(copy)
    norm_all[me] = norm_sum[...]

    arrived(back_copies)
    fine_rows(0)
    arrived(last_copies)
    sums = jnp.sum(jnp.sum(norm_all[...], axis=0), axis=1, keepdims=True)
    squares = jnp.broadcast_to(sums, (8, COARSE))
    step_ref[...] = squares / (squares + pltpu.roll(squares, 6, 0))
    arrived(back_copies_b)
    fine_rows(1)

    for copies in (
        out_copies,
        out_copies_b,
        sum_copies,
        sum_copies_b,
        edge_copies,
        edge_copies_b,
        share_copies,
        share_copies_b,
        norm_copies,
        last_copies,
        back_copies,
        back_copies_b,
    ):
        for copy in copies:
            copy.wait_send()


def per_device(residual, perturb, vertical_modes, column_weight, owner_table, column_map):
    vmem, dma = pltpu.VMEM, pltpu.SemaphoreType.DMA
    resid_part = residual[0]
    high = vertical_modes.astype(BF16)
    low = (vertical_modes - high.astype(F32)).astype(BF16)
    both = jnp.concatenate([jnp.pad(high, ((0, 0), (0, 6))), jnp.pad(low, ((0, 0), (0, 6)))], axis=1)
    whole = pl.BlockSpec(memory_space=pltpu.VMEM)
    anywhere = pl.BlockSpec(memory_space=pl.ANY)
    n = len(HOPS)
    fine, step = pl.pallas_call(
        kernel,
        out_shape=(
            jax.ShapeDtypeStruct((WIDE, FINE), BF16),
            jax.ShapeDtypeStruct((8, COARSE), F32),
        ),
        in_specs=[whole] * 5 + [anywhere] * 2,
        out_specs=(whole, whole),
        scratch_shapes=[
            vmem((2, FEAT, FINE), F32),
            vmem((MEMBERS, FEAT, COARSE), BF16),
            vmem((WIDE, FINE), F32),
            vmem((FINE, WIDE), BF16),
            vmem((REGIONS * CAP, FINE), BF16),
            vmem((FINE, REGIONS * CAP), BF16),
            vmem((REGIONS * CAP, COARSE), BF16),
            vmem((COARSE, REGIONS * CAP), BF16),
            vmem((REGIONS, CAP, OUT_CUT), BF16),
            vmem((REGIONS, CAP, WIDE - OUT_CUT), BF16),
            vmem((REGIONS, CAP, OUT_CUT), BF16),
            vmem((REGIONS, CAP, WIDE - OUT_CUT), BF16),
            vmem((WIDE, COARSE), F32),
            vmem((2 * ROWS, COARSE), F32),
            vmem((2, SLOTS - 1, SHARE, COARSE), F32),
            vmem((2, 2, 40, COARSE), F32),
            vmem((2, 2, 40, COARSE), F32),
            vmem((2, SHARE, COARSE), F32),
            vmem((2, SLOTS, SHARE, COARSE), BF16),
            vmem((16 * MEMBERS, COARSE), F32),
            vmem((WIDE, COARSE), F32),
            vmem((COARSE, WIDE), BF16),
            vmem((REGIONS, CAP, BACK_CUT), BF16),
            vmem((REGIONS, CAP, WIDE - BACK_CUT), BF16),
            vmem((REGIONS, CAP, BACK_CUT), BF16),
            vmem((REGIONS, CAP, WIDE - BACK_CUT), BF16),
            vmem((8, COARSE), F32),
            vmem((SLOTS - 1, 8, COARSE), F32),
            vmem((8, COARSE), F32),
            vmem((REGIONS, 8, COARSE), F32),
            dma((2,)),
            dma((2, n)),
            dma((2, n)),
            dma((2, n)),
            dma((2, n)),
            dma((2, 3)),
            dma((2, 3)),
            dma((2, 2)),
            dma((2, 2)),
            dma((2, 3)),
            dma((2, 3)),
            dma((3,)),
            dma((3,)),
            dma((n,)),
            dma((n,)),
        ],
        compiler_params=pltpu.CompilerParams(
            collective_id=0, has_side_effects=True, vmem_limit_bytes=60 * 2**20
        ),
        name="hessian",
    )(
        owner_table.reshape(REGIONS, FINE),
        column_map.reshape(REGIONS, FINE),
        column_weight.reshape(1, FINE),
        both.T,
        both,
        resid_part,
        perturb[0],
    )
    increment = jnp.stack([fine[0:FEAT], fine[FEAT_PAD : FEAT_PAD + FEAT]]).astype(F32)
    product = resid_part + increment * column_weight[None, None, :]
    step_length = step[0:2, 0]
    next_residual = resid_part - step_length[:, None, None] * product
    return (product[None], step_length, next_residual[None])


def solution(mesh):
    in_specs = (
        P("slot", None, None, "region"),
        P("slot", None, None, "region"),
        P(),
        P("region"),
        P(),
        P(),
    )
    out_specs = (P("slot", None, None, "region"), P(), P("slot", None, None, "region"))
    return jax.shard_map(
        per_device, mesh=mesh, in_specs=in_specs, out_specs=out_specs, check_vma=False
    )
```

profile of v0, /device:TPU:1, one launch (start us, length us, event | category | flops | bytes accessed | tf_op | source)
XLA Modules:
  0.0 155.2 jit_solution(2638110623042027291)
XLA Ops:
  0.6 0.9 fusion.4
  1.5 0.6 fusion.2
  2.1 0.5 broadcast.28
  2.7 1.6 %reduce.5 = s32[16384]{0:T(1024)S(1)} reduce(s32[16384,1]{0,1:T(1,128)} %param.10, s32[]{:T(128)} %broadcast.28), dimensions={1}, to_apply=%param.10.reduce_sub_computation.3 | reduce | bytes 131076 | tf_op args[4]
  4.3 0.6 reshape.55.owners_ref
  4.9 1.5 reshape.56.map_ref
  6.4 0.8 copy.29.modes_b_ref
  7.2 4.0 %copy.41 = f32[1,2,685,512]{3,2,1,0:T(8,128)} copy(f32[1,2,685,512]{3,1,2,0:T(2,128)} %param.6) | data formatting | bytes 5611520 | tf_op args[0]
  11.2 12.3 %copy.40 = bf16[1,64,685,128]{3,2,1,0:T(8,128)(2,1)} copy(bf16[1,64,685,128]{3,1,2,0:T(8,128)(2,1)} %param.7) | data formatting | bytes 22446080 | tf_op args[1]
  23.5 120.9 %hessian.1 = (bf16[1408,512]{1,0:T(8,128)(2,1)}, f32[8,128]{1,0:T(8,128)}) custom-call(s32[32,512]{1,0:T(8,128)} %reshape.55.owners_ref, s32[32,512]{1,0:T(8,128)} %reshape.56.map_ref, f32[1,512]{1,0:T(1,128)} %bitcast.16, bf16[32,685]{1,0:T(8,128)(2,1)} %get-tuple-element.21.modes_t_ref, bf16[685,32]{1,0:T(8,128)(2,1)} %copy.29.modes_b_ref, ...), custom_call_target="tpu_custom_call" | custom-call | tf_op jit(solution)/shard_map/hessian/pallas_call | solution.py:418
  144.4 0.0 copy-start
  144.5 0.0 copy-start.1
  144.5 1.6 %slice_bitcast_fusion.1 = (bf16[1,1,685,512]{3,2,1,0:T(8,128)(2,1)S(1)}, bf16[1,1,685,512]{3,2,1,0:T(8,128)(2,1)S(1)}) fusion(bf16[1408,512]{1,0:T(8,128)(2,1)} %get-tuple-element.5), kind=kLoop, calls=%fused_computation.5 | loop fusion | bytes 2805760 | tf_op jit(solution)/shard_map/stack | solution.py:486
  146.0 0.8 slice_reduce_fusion
  146.8 0.0 copy-done
  146.8 0.0 copy-done.1
  146.8 0.0 copy-start.2
  146.9 0.9 multiply_subtract_fusion
  147.8 0.0 copy-done.2
  147.8 3.7 %copy.33 = f32[1,2,685,512]{3,1,2,0:T(2,128)} copy(f32[1,2,685,512]{3,2,1,0:T(8,128)S(1)} %get-tuple-element.16) | data formatting | bytes 5611520
  151.5 3.7 %copy.32 = f32[1,2,685,512]{3,1,2,0:T(2,128)} copy(f32[1,2,685,512]{3,2,1,0:T(8,128)S(1)} %get-tuple-element.17) | data formatting | bytes 5611520
Async XLA Ops:
  144.4 2.4 %copy-start = (f32[1,2,685,512]{3,1,2,0:T(2,128)S(1)}, f32[1,2,685,512]{3,1,2,0:T(2,128)}, u32[]{:S(2)}) copy-start(f32[1,2,685,512]{3,1,2,0:T(2,128)} %param.6) | copy-start | bytes 8417284
  144.5 2.4 %copy-start.1 = (f32[512]{0:T(512)S(1)}, f32[512]{0:T(512)}, u32[]{:S(2)}) copy-start(f32[512]{0:T(512)} %param.9) | copy-start | bytes 6148
  146.8 1.0 copy-start.2
where the time goes:
time: 156 us; the launch traced here: 155 us
  Pallas kernels  121 us (78%)
  local copies, waits for them, and re-layouts  29.5 us (19%)
  other arithmetic  4.1 us (3%)
    pallas_call x1, Pallas kernels, per_device(): pl.pallas_call(kernel, out_shape=(jax.ShapeDtypeStruct((WIDE, FINE), BF16...  121 us
    unnamed x11, local copies, waits for them, and re-layouts  24.3 us

commit v1 on v0

--- a/solution.py
+++ b/solution.py
@@ -17,7 +17,7 @@
 FINE = 512
 COARSE = 128
 FEAT = 685
-FEAT_PAD = 688
+FEAT_PAD = 704
 WIDE = 1408
 MEMBERS = 64
 MODES = 10
@@ -25,6 +25,10 @@
 SHARE = ROWS // SLOTS
 OUT_CUT = 768
 BACK_CUT = 640
+GROUP = 8
+GROUPS = MEMBERS // GROUP
+SPREAD = MODES * GROUP
+STEP = 64
 
 NEAR_FIRST = (
     [(0, 1), (1, 0), (0, 3), (3, 0)],
@@ -55,11 +59,10 @@
     owners_ref,
     map_ref,
     weight_ref,
-    modes_t_ref,
-    modes_b_ref,
+    modes_ref,
     resid_hbm,
     members_hbm,
-    fine_ref,
+    fine_hbm,
     step_ref,
     resid,
     members,
@@ -74,19 +77,24 @@
     recv_a,
     recv_b,
     coarse,
+    modes_rep,
+    mixer,
+    mixer_t,
+    gathered_modes,
+    mode_cells,
     control,
     summed_in,
     edge_out,
     edge_in,
     shares,
     gathered,
-    smoothed,
     total,
     total_t,
     back_a,
     back_b,
     home_a,
     home_b,
+    fine,
     norm,
     norm_in,
     norm_sum,
@@ -116,9 +124,10 @@
         return (((z + dz) % 4) * 4 + (x + dx) % 4) * 2 + (core + dc) % 2
 
     partners = [region_at(h) for h in HOPS]
-    load_resid = pltpu.make_async_copy(resid_hbm, resid, load_sem.at[0])
-    load_resid.start()
-    load_members = pltpu.make_async_copy(members_hbm, members, load_sem.at[1])
+    load_resid = [pltpu.make_async_copy(resid_hbm.at[:, v, :], resid.at[v], load_sem.at[v]) for v in range(2)]
+    for copy in load_resid:
+        copy.start()
+    load_members = pltpu.make_async_copy(members_hbm, members.at[pl.ds(0, FEAT)], load_sem.at[2])
     load_members.start()
 
     barrier = pltpu.get_barrier_semaphore()
@@ -127,7 +136,8 @@
     for d in (1, 2, 3):
         pl.semaphore_signal(barrier, inc=1, device_id={"slot": (slot + d) % SLOTS}, device_id_type=MESH)
 
-    own = owners_ref[pl.ds(me, 1), :]
+    mine = pl.ds(pl.multiple_of(me * FINE, FINE), FINE)
+    own = owners_ref[:, mine]
     owner_hot = (lax.broadcasted_iota(jnp.int32, (REGIONS, FINE), 0) == own).astype(BF16)
     earlier = (
         lax.broadcasted_iota(jnp.int32, (FINE, FINE), 0) < lax.broadcasted_iota(jnp.int32, (FINE, FINE), 1)
@@ -140,12 +150,13 @@
         hot = lax.broadcasted_iota(jnp.int32, (256, FINE), 0) + q * 256 == my_slots
         slot_hot_t[rows, :] = hot.astype(F32).astype(BF16)
 
-    wide_rows[pl.ds(1373, WIDE - 1373), :] = jnp.zeros((WIDE - 1373, FINE), F32)
-    index_row = (map_ref[pl.ds(me, 1), :] + 1).astype(F32)
-    wide_rows[pl.ds(FEAT, 3), :] = jnp.broadcast_to(index_row, (3, FINE))
-    load_resid.wait()
+    index_row = (map_ref[:, mine] + 1).astype(F32)
+    spare = FEAT_PAD - FEAT
+    wide_rows[pl.ds(FEAT, spare), :] = jnp.broadcast_to(index_row, (spare, FINE))
+    wide_rows[pl.ds(FEAT_PAD + FEAT, spare), :] = jnp.zeros((spare, FINE), F32)
     norm[...] = jnp.zeros_like(norm)
     for v in range(2):
+        load_resid[v].wait()
         field = resid[v]
         wide_rows[pl.ds(v * FEAT_PAD, FEAT), :] = field * weight_ref[...]
         by_col = jnp.sum(field * field, axis=0, keepdims=True)
@@ -185,24 +196,56 @@
     out_copies_b = exchange(send_b, recv_b, 1, out_send, out_recv)
 
     slot_hot[...] = slot_hot_t[...].T
-    total[...] = jnp.zeros_like(total)
-    smoothed[...] = jnp.zeros_like(smoothed)
+    members[pl.ds(FEAT, spare)] = jnp.zeros((spare, MEMBERS, COARSE), BF16)
+
+    repeat = (
+        lax.broadcasted_iota(jnp.int32, (SPREAD, MODES), 0) // GROUP
+        == lax.broadcasted_iota(jnp.int32, (SPREAD, MODES), 1)
+    ).astype(F32).astype(BF16)
+    high = modes_ref[...].astype(BF16)
+    low = (modes_ref[...] - high.astype(F32)).astype(BF16)
+    modes_rep[...] = jnp.zeros_like(modes_rep)
+    modes_rep[pl.ds(0, FEAT), :] = jnp.concatenate([dot(repeat, high), dot(repeat, low)], axis=0).T
+
+    def mixer_step(i, carry):
+        cut = (32, GROUP, 2 * SPREAD)
+        rows = modes_rep[pl.ds(pl.multiple_of(i * 32, 32), 32), :]
+        same = lax.broadcasted_iota(jnp.int32, cut, 1) == lax.broadcasted_iota(jnp.int32, cut, 2) % GROUP
+        block = jnp.where(same, jnp.broadcast_to(rows[:, None, :], cut), 0.0).reshape(256, 2 * SPREAD)
+        at = pl.ds(pl.multiple_of(i * 256, 256), 256)
+        mixer[at, :] = block.astype(BF16)
+        mixer_t[:, at] = block.T.astype(BF16)
+        return carry
+
+    lax.fori_loop(0, FEAT_PAD // 32, mixer_step, 0)
     load_members.wait()
 
     def contract(v):
-        field = coarse[pl.ds(v * FEAT_PAD, FEAT), :]
-
-        def pair(i, carry):
-            halves = [(members[2 * i + e].astype(F32) * field).astype(BF16) for e in range(2)]
-            got = dot(modes_t_ref[...], jnp.concatenate(halves, axis=1))
-            got = got[0:16] + got[16:32]
-            for e in range(2):
-                control[pl.ds(v * ROWS + 2 * i + e, MODES, stride=MEMBERS), :] = got[
-                    0:MODES, e * COARSE : (e + 1) * COARSE
+        gathered_modes[...] = jnp.zeros_like(gathered_modes)
+
+        def chunk(i, carry):
+            field = coarse[pl.ds(pl.multiple_of(v * FEAT_PAD + i * STEP, STEP), STEP), :]
+            cells = members[pl.ds(i * STEP, STEP)].astype(F32).reshape(STEP, GROUPS, GROUP, COARSE)
+            product = cells * field[:, None, None, :]
+            left = mixer_t[:, pl.ds(pl.multiple_of(i * STEP * GROUP, STEP * GROUP), STEP * GROUP)]
+            for pair in range(GROUPS // 2):
+                both = jnp.concatenate(
+                    [product[:, 2 * pair + e].reshape(STEP * GROUP, COARSE) for e in range(2)], axis=1
+                )
+                top = both.astype(BF16)
+                rest = (both - top.astype(F32)).astype(BF16)
+                main = dot(left, top)
+                gathered_modes[:, pair * 256 : (pair + 1) * 256] += (
+                    main[0:SPREAD] + main[SPREAD:] + dot(left[0:SPREAD], rest)
+                )
+            return carry
+
+        lax.fori_loop(0, FEAT_PAD // STEP, chunk, 0)
+        for m in range(MODES):
+            for g in range(GROUPS):
+                control[pl.ds(v * ROWS + m * MEMBERS + g * GROUP, GROUP), :] = gathered_modes[
+                    m * GROUP : (m + 1) * GROUP, g * COARSE : (g + 1) * COARSE
                 ]
-            return carry
-
-        lax.fori_loop(0, MEMBERS // 2, pair, 0)
 
     def share_rows(v, t):
         return pl.ds(pl.multiple_of(v * ROWS + t * SHARE, 8), SHARE)
@@ -281,23 +324,28 @@
         return copies
 
     def expand(v):
-        for t in range(SLOTS):
-            smoothed[pl.ds(t * SHARE, SHARE), :] = gathered[v, t].astype(F32)
-
-        def pair(i, carry):
-            halves = []
-            for e in range(2):
-                cells = smoothed[pl.ds(2 * i + e, 16, stride=MEMBERS), :].astype(BF16)
-                halves.append(jnp.concatenate([cells, cells], axis=0))
-            mixed = dot(modes_b_ref[...], jnp.concatenate(halves, axis=1))
-            total[pl.ds(v * FEAT_PAD, FEAT), :] += (
-                members[2 * i].astype(F32) * mixed[:, 0:COARSE]
-                + members[2 * i + 1].astype(F32) * mixed[:, COARSE : 2 * COARSE]
-            )
+        every = jnp.concatenate([gathered[v, t].astype(F32) for t in range(SLOTS)], axis=0)
+        for g in range(GROUPS):
+            cells = jnp.concatenate(
+                [every[m * MEMBERS + g * GROUP : m * MEMBERS + (g + 1) * GROUP] for m in range(MODES)], axis=0
+            ).astype(BF16)
+            mode_cells[0:SPREAD, g * COARSE : (g + 1) * COARSE] = cells
+            mode_cells[SPREAD:, g * COARSE : (g + 1) * COARSE] = cells
+
+        def chunk(i, carry):
+            left = mixer[pl.ds(pl.multiple_of(i * STEP * GROUP, STEP * GROUP), STEP * GROUP), :]
+            cells = members[pl.ds(i * STEP, STEP)].astype(F32).reshape(STEP, GROUPS, GROUP, COARSE)
+            sums = jnp.zeros((STEP, GROUP, COARSE), F32)
+            for pair in range(GROUPS // 2):
+                mixed = dot(left, mode_cells[:, pair * 256 : (pair + 1) * 256])
+                for e in range(2):
+                    part = mixed[:, e * COARSE : (e + 1) * COARSE].reshape(STEP, GROUP, COARSE)
+                    sums = sums + cells[:, 2 * pair + e] * part
+            at = pl.ds(pl.multiple_of(v * FEAT_PAD + i * STEP, STEP), STEP)
+            total[at, :] = jnp.sum(sums, axis=1)
             return carry
 
-        lax.fori_loop(0, MEMBERS // 2, pair, 0)
-
+        lax.fori_loop(0, FEAT_PAD // STEP, chunk, 0)
 
     def arrived(copies):
         for copy in copies:
@@ -315,7 +363,12 @@
         home = (home_a, home_b)[chunk][...].reshape(REGIONS * CAP, width)
         for q in range(4):
             got = dot(slot_hot[pl.ds(q * 128, 128), :], home)
-            fine_ref[pl.ds(left, width), q * 128 : (q + 1) * 128] = got.T.astype(BF16)
+            rows, cols = got.T, slice(q * 128, (q + 1) * 128)
+            if chunk == 0:
+                fine[0, 0:BACK_CUT, cols] = rows
+            else:
+                fine[0, BACK_CUT:FEAT, cols] = rows[0 : FEAT - BACK_CUT]
+                fine[1, :, cols] = rows[FEAT_PAD - BACK_CUT : FEAT_PAD - BACK_CUT + FEAT]
 
     arrived(out_copies)
     sent = recv_a[...].reshape(REGIONS * CAP, OUT_CUT)
@@ -326,6 +379,7 @@
     place[...] = hot.astype(F32).astype(BF16)
     place_t[...] = place[...].T
     coarse[pl.ds(0, OUT_CUT), :] = dot(place_t[...], sent).T
+    total[pl.ds(FEAT_PAD, FEAT_PAD), :] = jnp.zeros((FEAT_PAD, COARSE), F32)
     contract(0)
     sum_copies = sum_start(0)
     arrived(sum_copies)
@@ -387,6 +441,14 @@
     step_ref[...] = squares / (squares + pltpu.roll(squares, 6, 0))
     arrived(back_copies_b)
     fine_rows(1)
+    stores = [
+        pltpu.make_async_copy(fine.at[v], fine_hbm.at[:, v, :], load_sem.at[v])
+        for v in range(2)
+    ]
+    for copy in stores:
+        copy.start()
+    for copy in stores:
+        copy.wait()
 
     for copies in (
         out_copies,
@@ -406,26 +468,31 @@
             copy.wait_send()
 
 
+def last_step(resid_ref, increment_ref, weight_ref, step_ref, product_ref, next_ref):
+    step = jnp.concatenate([step_ref[0:2, :]] * 4, axis=1)[None]
+    product = resid_ref[...] + increment_ref[...] * weight_ref[...][None]
+    product_ref[...] = product
+    next_ref[...] = resid_ref[...] - step * product
+
+
 def per_device(residual, perturb, vertical_modes, column_weight, owner_table, column_map):
     vmem, dma = pltpu.VMEM, pltpu.SemaphoreType.DMA
-    resid_part = residual[0]
-    high = vertical_modes.astype(BF16)
-    low = (vertical_modes - high.astype(F32)).astype(BF16)
-    both = jnp.concatenate([jnp.pad(high, ((0, 0), (0, 6))), jnp.pad(low, ((0, 0), (0, 6)))], axis=1)
+    resid_part = residual[0].transpose(1, 0, 2)
+    weight = column_weight.reshape(1, FINE)
     whole = pl.BlockSpec(memory_space=pltpu.VMEM)
     anywhere = pl.BlockSpec(memory_space=pl.ANY)
     n = len(HOPS)
-    fine, step = pl.pallas_call(
+    increment, step = pl.pallas_call(
         kernel,
         out_shape=(
-            jax.ShapeDtypeStruct((WIDE, FINE), BF16),
+            jax.ShapeDtypeStruct((FEAT, 2, FINE), F32),
             jax.ShapeDtypeStruct((8, COARSE), F32),
         ),
-        in_specs=[whole] * 5 + [anywhere] * 2,
-        out_specs=(whole, whole),
+        in_specs=[whole] * 4 + [anywhere] * 2,
+        out_specs=(anywhere, whole),
         scratch_shapes=[
             vmem((2, FEAT, FINE), F32),
-            vmem((MEMBERS, FEAT, COARSE), BF16),
+            vmem((FEAT_PAD, MEMBERS, COARSE), BF16),
             vmem((WIDE, FINE), F32),
             vmem((FINE, WIDE), BF16),
             vmem((REGIONS * CAP, FINE), BF16),
@@ -437,24 +504,29 @@
             vmem((REGIONS, CAP, OUT_CUT), BF16),
             vmem((REGIONS, CAP, WIDE - OUT_CUT), BF16),
             vmem((WIDE, COARSE), F32),
+            vmem((FEAT_PAD, 2 * SPREAD), F32),
+            vmem((FEAT_PAD * GROUP, 2 * SPREAD), BF16),
+            vmem((2 * SPREAD, FEAT_PAD * GROUP), BF16),
+            vmem((SPREAD, GROUPS * COARSE), F32),
+            vmem((2 * SPREAD, GROUPS * COARSE), BF16),
             vmem((2 * ROWS, COARSE), F32),
             vmem((2, SLOTS - 1, SHARE, COARSE), F32),
             vmem((2, 2, 40, COARSE), F32),
             vmem((2, 2, 40, COARSE), F32),
             vmem((2, SHARE, COARSE), F32),
             vmem((2, SLOTS, SHARE, COARSE), BF16),
-            vmem((16 * MEMBERS, COARSE), F32),
             vmem((WIDE, COARSE), F32),
             vmem((COARSE, WIDE), BF16),
             vmem((REGIONS, CAP, BACK_CUT), BF16),
             vmem((REGIONS, CAP, WIDE - BACK_CUT), BF16),
             vmem((REGIONS, CAP, BACK_CUT), BF16),
             vmem((REGIONS, CAP, WIDE - BACK_CUT), BF16),
+            vmem((2, FEAT, FINE), F32),
             vmem((8, COARSE), F32),
             vmem((SLOTS - 1, 8, COARSE), F32),
             vmem((8, COARSE), F32),
             vmem((REGIONS, 8, COARSE), F32),
-            dma((2,)),
+            dma((3,)),
             dma((2, n)),
             dma((2, n)),
             dma((2, n)),
@@ -475,19 +547,28 @@
         ),
         name="hessian",
     )(
-        owner_table.reshape(REGIONS, FINE),
-        column_map.reshape(REGIONS, FINE),
-        column_weight.reshape(1, FINE),
-        both.T,
-        both,
+        owner_table.reshape(1, REGIONS * FINE),
+        column_map.reshape(1, REGIONS * FINE),
+        weight,
+        vertical_modes.T,
         resid_part,
-        perturb[0],
+        perturb[0].transpose(1, 0, 2),
     )
-    increment = jnp.stack([fine[0:FEAT], fine[FEAT_PAD : FEAT_PAD + FEAT]]).astype(F32)
-    product = resid_part + increment * column_weight[None, None, :]
-    step_length = step[0:2, 0]
-    next_residual = resid_part - step_length[:, None, None] * product
-    return (product[None], step_length, next_residual[None])
+    block = pl.BlockSpec((137, 2, FINE), lambda i: (i, 0, 0))
+    product, next_residual = pl.pallas_call(
+        last_step,
+        grid=(FEAT // 137,),
+        out_shape=(jax.ShapeDtypeStruct((FEAT, 2, FINE), F32),) * 2,
+        in_specs=[
+            block,
+            block,
+            pl.BlockSpec((1, FINE), lambda i: (0, 0)),
+            pl.BlockSpec((8, COARSE), lambda i: (0, 0)),
+        ],
+        out_specs=(block, block),
+        name="last_step",
+    )(resid_part, increment, weight, step)
+    return (product.transpose(1, 0, 2)[None], step[0:2, 0], next_residual.transpose(1, 0, 2)[None])
 
 
 def solution(mesh):

time: 156 us -> 127 us (0.81)
  local copies, waits for them, and re-layouts: 29.5 us -> 1.3 us
  other arithmetic: 4.1 us -> 0 us
  Pallas kernels: 121 us -> 124 us
    unnamed x11 -> x0, local copies, waits for them, and re-layouts: 24.3 us -> none
    pallas_call x1 -> x2, Pallas kernels: 121 us -> 124 us  [the longest x1 117 us: per_device(): pl.pallas_call(kernel, out_shape=(jax.ShapeDtypeStruct((FEAT, 2, FINE), F...]
    reshape x2 -> x0, local copies, waits for them, and re-layouts: 2.12 us -> none  [the longest x1 1.48 us: per_device(): column_map.reshape(REGIONS, FINE)]
    unnamed x1 -> x0, other arithmetic: 1.64 us -> none
    another operation x1 -> x0, local copies, waits for them, and re-layouts: 1.56 us -> none  [per_device(): jnp.stack([fine[0:FEAT], fine[FEAT_PAD:FEAT_PAD + FEAT]]).astype(F32)]
where the time goes in v1:
time: 127 us; the launch traced here: 126 us
  Pallas kernels  124 us (98%)
  local copies, waits for them, and re-layouts  1.3 us (1%)
    pallas_call x1, Pallas kernels, per_device(): pl.pallas_call(kernel, out_shape=(jax.ShapeDtypeStruct((FEAT, 2, FINE), F...  117 us
    pallas_call x1, Pallas kernels, per_device(): pl.pallas_call(last_step, grid=(FEAT // 137,), out_shape=(jax.ShapeDtypeS...  6.78 us

profile of v1, /device:TPU:1, one launch (start us, length us, event | category | flops | bytes accessed | tf_op | source)
XLA Modules:
  0.0 125.8 jit_solution(4961778053216536484)
XLA Ops:
  0.6 117.1 %hessian.1 = (f32[685,2,512]{2,1,0:T(2,128)}, f32[8,128]{1,0:T(8,128)}) custom-call(s32[1,16384]{1,0:T(1,128)} %bitcast.19, s32[1,16384]{1,0:T(1,128)} %bitcast.20, f32[1,512]{1,0:T(1,128)} %bitcast.22, f32[10,685]{1,0:T(8,128)} %bitcast.21, f32[685,2,512]{2,1,0:T(2,128)} %bitcast.17, bf16[685,64,128]{2,1,0:T(8,128)(2,1)} %bitcast.16), custom_call_target="tpu_custom_call" | custom-call | tf_op jit(solution)/shard_map/hessian/pallas_call | solution.py:485
  117.7 6.8 %last_step.1 = (f32[685,2,512]{2,1,0:T(2,128)}, f32[685,2,512]{2,1,0:T(2,128)}) custom-call(f32[685,2,512]{2,1,0:T(2,128)} %bitcast.18, f32[685,2,512]{2,1,0:T(2,128)} %get-tuple-element.7.increment_ref, f32[1,512]{1,0:T(1,128)} %bitcast.23, f32[8,128]{1,0:T(8,128)} %get-tuple-element.8.step_ref), custom_call_target="tpu_custom_call" | custom-call | tf_op jit(solution)/shard_map/last_step/pallas_call | solution.py:558
  124.5 1.3 %slice_reduce_fusion = f32[2]{0:T(128)} fusion(f32[8,128]{1,0:T(8,128)} %get-tuple-element.8.step_ref), kind=kLoop, calls=%fused_computation | loop fusion | bytes 16 | tf_op jit(solution)/shard_map/slice | solution.py:571

commit v2 on v1

--- a/solution.py
+++ b/solution.py
@@ -23,12 +23,13 @@
 MODES = 10
 ROWS = MODES * MEMBERS
 SHARE = ROWS // SLOTS
-OUT_CUT = 768
-BACK_CUT = 640
+OUT = ((0, 384, 0), (384, 384, 1), (768, 384, 0), (1152, 256, 1))
+BACK = ((0, 384, 0), (384, 256, 1), (640, 384, 0), (1024, 384, 1))
+LINE = ((2, 0), (2, 1), (1, 0), (3, 0), (1, 1), (3, 1), (0, 1))
 GROUP = 8
 GROUPS = MEMBERS // GROUP
 SPREAD = MODES * GROUP
-STEP = 64
+STEP = 176
 
 NEAR_FIRST = (
     [(0, 1), (1, 0), (0, 3), (3, 0)],
@@ -62,7 +63,8 @@
     modes_ref,
     resid_hbm,
     members_hbm,
-    fine_hbm,
+    product_hbm,
+    next_hbm,
     step_ref,
     resid,
     members,
@@ -70,12 +72,14 @@
     wide_cols,
     slot_hot_t,
     slot_hot,
+    index_out,
+    index_in,
     place,
     place_t,
-    send_a,
-    send_b,
-    recv_a,
-    recv_b,
+    send,
+    middle,
+    part,
+    part_in,
     coarse,
     modes_rep,
     mixer,
@@ -89,19 +93,25 @@
     shares,
     gathered,
     total,
-    total_t,
-    back_a,
-    back_b,
-    home_a,
-    home_b,
+    spread_out,
+    spread_in,
+    back,
+    home,
     fine,
+    stepped,
     norm,
     norm_in,
     norm_sum,
     norm_all,
     load_sem,
+    index_send,
+    index_recv,
     out_send,
     out_recv,
+    part_send,
+    part_recv,
+    spread_send,
+    spread_recv,
     back_send,
     back_recv,
     sum_send,
@@ -127,8 +137,6 @@
     load_resid = [pltpu.make_async_copy(resid_hbm.at[:, v, :], resid.at[v], load_sem.at[v]) for v in range(2)]
     for copy in load_resid:
         copy.start()
-    load_members = pltpu.make_async_copy(members_hbm, members.at[pl.ds(0, FEAT)], load_sem.at[2])
-    load_members.start()
 
     barrier = pltpu.get_barrier_semaphore()
     for p in partners:
@@ -144,58 +152,148 @@
     ).astype(BF16)
     before = dot(owner_hot, earlier)
     rank = jnp.sum(owner_hot.astype(F32) * before, axis=0, keepdims=True)
-    my_slots = own * CAP + rank.astype(jnp.int32)
+    rank = rank.astype(jnp.int32)
+    own_z, own_x, own_core = own // 8, (own // 2) % 4, own % 2
+    index_row = (map_ref[:, mine] + 1).astype(F32)
+    index_rows = jnp.broadcast_to(index_row, (16, FINE)).astype(BF16)
+    for mode, (first, second) in enumerate(((own_z, own_x), (own_x, own_z))):
+        my_slots = (first * 2 + own_core) * 128 + second * CAP + rank
+        for q in range(4):
+            hot = lax.broadcasted_iota(jnp.int32, (256, FINE), 0) + q * 256 == my_slots
+            hot = hot.astype(F32).astype(BF16)
+            slot_hot_t[mode, pl.ds(q * 256, 256), :] = hot
+            got = lax.dot_general(
+                index_rows, hot, (((1,), (1,)), ((), ())), preferred_element_type=F32
+            ).astype(BF16)
+            for e in range(2):
+                index_out[mode, 2 * q + e] = got[:, e * 128 : (e + 1) * 128]
+
+    spare = FEAT_PAD - FEAT
+    wide_rows[pl.ds(FEAT, spare), :] = jnp.zeros((spare, FINE), F32)
+    wide_rows[pl.ds(FEAT_PAD + FEAT, spare), :] = jnp.zeros((spare, FINE), F32)
+    for v in range(2):
+        load_resid[v].wait()
+        wide_rows[pl.ds(v * FEAT_PAD, FEAT), :] = resid[v] * weight_ref[...]
+    load_members = pltpu.make_async_copy(members_hbm, members.at[pl.ds(0, FEAT)], load_sem.at[2])
+    load_members.start()
     for q in range(4):
-        rows = pl.ds(q * 256, 256)
-        hot = lax.broadcasted_iota(jnp.int32, (256, FINE), 0) + q * 256 == my_slots
-        slot_hot_t[rows, :] = hot.astype(F32).astype(BF16)
-
-    index_row = (map_ref[:, mine] + 1).astype(F32)
-    spare = FEAT_PAD - FEAT
-    wide_rows[pl.ds(FEAT, spare), :] = jnp.broadcast_to(index_row, (spare, FINE))
-    wide_rows[pl.ds(FEAT_PAD + FEAT, spare), :] = jnp.zeros((spare, FINE), F32)
+        wide_cols[pl.ds(q * 128, 128), :] = wide_rows[:, q * 128 : (q + 1) * 128].T.astype(BF16)
+
+    pl.semaphore_wait(barrier, len(HOPS) + 3)
+
+    def spot(mode):
+        return (z, x) if mode == 0 else (x, z)
+
+    def device_at(mode, a, b, c):
+        return ((a * 4 + b) if mode == 0 else (b * 4 + a)) * 2 + c
+
+    def push(source, landing, send_sem, recv_sem, target):
+        copy = pltpu.make_async_remote_copy(
+            src_ref=source,
+            dst_ref=landing,
+            send_sem=send_sem,
+            recv_sem=recv_sem,
+            device_id=target,
+            device_id_type=MESH,
+        )
+        copy.start()
+        return copy
+
+    def line_peers(mode):
+        a, b = spot(mode)
+        for j, (da, dc) in enumerate(LINE):
+            a_to, c_to = (a + da) % 4, (core + dc) % 2
+            yield j, a_to * 2 + c_to, {"region": device_at(mode, a_to, b, c_to)}
+
+    def cross_peers(mode):
+        a, b = spot(mode)
+        for j, db in enumerate((2, 1, 3)):
+            b_to = (b + db) % 4
+            yield j, b_to, {"region": device_at(mode, a, b_to, core)}
+
+    def pack(piece):
+        left, width, mode = OUT[piece]
+
+        def one(q, carry):
+            rows = slot_hot_t[mode, pl.ds(pl.multiple_of(q * 256, 256), 256), :]
+            got = dot(rows, wide_cols[:, left : left + width])
+            send[piece][pl.ds(q * 2, 2)] = got.astype(BF16).reshape(2, 4, CAP, width)
+            return carry
+
+        lax.fori_loop(0, 4, one, 0)
+
+    def out_start(piece, ahead):
+        mode = OUT[piece][2]
+        here = spot(mode)[0] * 2 + core
+        copies = []
+        for j, there, target in line_peers(mode):
+            if ahead is not None:
+                ahead[j].wait_send()
+            copies.append(
+                push(
+                    send[piece].at[there],
+                    middle[piece].at[:, here],
+                    out_send.at[piece, j],
+                    out_recv.at[piece, j],
+                    target,
+                )
+            )
+        middle[piece][:, here] = send[piece][here]
+        return copies
+
+    def part_start(piece):
+        mode = OUT[piece][2]
+        here = spot(mode)[1]
+        for b in range(4):
+            rows = middle[piece][b].reshape(8 * CAP, OUT[piece][1])
+            part[piece][b] = dot(place_t[mode, b], rows).astype(BF16)
+        copies = [
+            push(
+                part[piece].at[there],
+                part_in[piece].at[here],
+                part_send.at[piece, j],
+                part_recv.at[piece, j],
+                target,
+            )
+            for j, there, target in cross_peers(mode)
+        ]
+        part_in[piece][here] = part[piece][here]
+        return copies
+
+    def coarse_rows(piece):
+        left, width, _ = OUT[piece]
+        sums = part_in[piece][0].astype(F32)
+        for b in range(1, 4):
+            sums = sums + part_in[piece][b].astype(F32)
+        coarse[pl.ds(left, width), :] = sums.T
+
+    index_copies = []
+    for mode in range(2):
+        here = spot(mode)[0] * 2 + core
+        for j, there, target in line_peers(mode):
+            index_copies.append(
+                push(
+                    index_out.at[mode, there],
+                    index_in.at[mode, here],
+                    index_send.at[mode, j],
+                    index_recv.at[mode, j],
+                    target,
+                )
+            )
+        index_in[mode, here] = index_out[mode, here]
+    pack(0)
+    out_0 = out_start(0, None)
+    pack(1)
+    out_1 = out_start(1, None)
+    pack(2)
+    pack(3)
+
     norm[...] = jnp.zeros_like(norm)
     for v in range(2):
-        load_resid[v].wait()
-        field = resid[v]
-        wide_rows[pl.ds(v * FEAT_PAD, FEAT), :] = field * weight_ref[...]
-        by_col = jnp.sum(field * field, axis=0, keepdims=True)
+        by_col = jnp.sum(resid[v] * resid[v], axis=0, keepdims=True)
         norm[pl.ds(v, 1), :] = by_col[:, 0:128] + by_col[:, 128:256] + by_col[:, 256:384] + by_col[:, 384:512]
-    for q in range(4):
-        wide_cols[pl.ds(q * 128, 128), :] = wide_rows[:, q * 128 : (q + 1) * 128].T.astype(BF16)
-
-    pl.semaphore_wait(barrier, len(HOPS) + 3)
-
-    def pack(out, left, matrix, depth_rows, width):
-        def one(q, carry):
-            got = dot(matrix[pl.ds(pl.multiple_of(q * 256, 256), 256), :], depth_rows[:, left : left + width])
-            out[pl.ds(q * 8, 8)] = got.astype(BF16).reshape(8, CAP, width)
-            return carry
-
-        lax.fori_loop(0, 4, one, 0)
-
-    def exchange(source, landing, chunk, send_sems, recv_sems):
-        copies = []
-        for i, p in enumerate(partners):
-            copy = pltpu.make_async_remote_copy(
-                src_ref=source.at[p],
-                dst_ref=landing.at[me],
-                send_sem=send_sems.at[chunk, i],
-                recv_sem=recv_sems.at[chunk, i],
-                device_id={"region": p},
-                device_id_type=MESH,
-            )
-            copy.start()
-            copies.append(copy)
-        landing[me] = source[me]
-        return copies
-
-    pack(send_a, 0, slot_hot_t, wide_cols, OUT_CUT)
-    out_copies = exchange(send_a, recv_a, 0, out_send, out_recv)
-    pack(send_b, OUT_CUT, slot_hot_t, wide_cols, WIDE - OUT_CUT)
-    out_copies_b = exchange(send_b, recv_b, 1, out_send, out_recv)
-
-    slot_hot[...] = slot_hot_t[...].T
+    for mode in range(2):
+        slot_hot[mode] = slot_hot_t[mode].T
     members[pl.ds(FEAT, spare)] = jnp.zeros((spare, MEMBERS, COARSE), BF16)
 
     repeat = (
@@ -218,6 +316,28 @@
         return carry
 
     lax.fori_loop(0, FEAT_PAD // 32, mixer_step, 0)
+
+    for copy in index_copies:
+        copy.wait_recv()
+    lane = lax.broadcasted_iota(jnp.int32, (8, COARSE), 1)
+    for mode in range(2):
+        tables = [index_in[mode, p].astype(F32)[0:8] for p in range(8)]
+        for b in range(4):
+            halves = []
+            for h in range(2):
+                row = jnp.zeros((8, COARSE), F32)
+                for g in range(4):
+                    shift = (g - b) * CAP % COARSE
+                    table = tables[h * 4 + g]
+                    row = jnp.where(lane // CAP == g, pltpu.roll(table, shift, 1) if shift else table, row)
+                halves.append(row[0:1])
+            row = jnp.concatenate(halves, axis=1)
+            hot = (lax.broadcasted_iota(jnp.int32, (COARSE, 8 * CAP), 0) + 1).astype(F32) == row
+            hot = hot.astype(F32)
+            place_t[mode, b] = hot.astype(BF16)
+            place[mode, b] = hot.T.astype(BF16)
+    out_2 = out_start(2, out_0)
+    out_3 = out_start(3, out_1)
     load_members.wait()
 
     def contract(v):
@@ -351,55 +471,103 @@
         for copy in copies:
             copy.wait_recv()
 
-    def back_start(chunk):
-        left, width = ((0, BACK_CUT), (BACK_CUT, WIDE - BACK_CUT))[chunk]
-        out = (back_a, back_b)[chunk]
-        total_t[:, left : left + width] = total[pl.ds(left, width), :].T.astype(BF16)
-        pack(out, left, place, total_t, width)
-        return exchange(out, (home_a, home_b)[chunk], chunk, back_send, back_recv)
-
-    def fine_rows(chunk):
-        left, width = ((0, BACK_CUT), (BACK_CUT, WIDE - BACK_CUT))[chunk]
-        home = (home_a, home_b)[chunk][...].reshape(REGIONS * CAP, width)
+    def spread_start(piece):
+        left, width, mode = BACK[piece]
+        here = spot(mode)[1]
+        spread_out[piece][...] = total[pl.ds(left, width), :].T.astype(BF16)
+        copies = [
+            push(
+                spread_out[piece],
+                spread_in[piece].at[here],
+                spread_send.at[piece, j],
+                spread_recv.at[piece, j],
+                target,
+            )
+            for j, _, target in cross_peers(mode)
+        ]
+        spread_in[piece][here] = spread_out[piece][...]
+        return copies
+
+    def back_start(piece):
+        _, width, mode = BACK[piece]
+        here = spot(mode)[0] * 2 + core
+        for b in range(4):
+            rows = dot(place[mode, b], spread_in[piece][b])
+            back[piece][:, b] = rows.astype(BF16).reshape(8, CAP, width)
+        copies = [
+            push(
+                back[piece].at[there],
+                home[piece].at[here],
+                back_send.at[piece, j],
+                back_recv.at[piece, j],
+                target,
+            )
+            for j, there, target in line_peers(mode)
+        ]
+        home[piece][here] = back[piece][here]
+        return copies
+
+    def fine_rows(piece):
+        left, width, mode = BACK[piece]
+        source = home[piece][...].reshape(REGIONS * CAP, width)
         for q in range(4):
-            got = dot(slot_hot[pl.ds(q * 128, 128), :], home)
-            rows, cols = got.T, slice(q * 128, (q + 1) * 128)
-            if chunk == 0:
-                fine[0, 0:BACK_CUT, cols] = rows
-            else:
-                fine[0, BACK_CUT:FEAT, cols] = rows[0 : FEAT - BACK_CUT]
-                fine[1, :, cols] = rows[FEAT_PAD - BACK_CUT : FEAT_PAD - BACK_CUT + FEAT]
-
-    arrived(out_copies)
-    sent = recv_a[...].reshape(REGIONS * CAP, OUT_CUT)
-    near = sent[:, 640:768].astype(F32)
-    lane = lax.broadcasted_iota(jnp.int32, (REGIONS * CAP, COARSE), 1)
-    index = jnp.sum(jnp.where(lane == FEAT - 640, near, 0.0), axis=1, keepdims=True)
-    hot = (lane + 1).astype(F32) == index
-    place[...] = hot.astype(F32).astype(BF16)
-    place_t[...] = place[...].T
-    coarse[pl.ds(0, OUT_CUT), :] = dot(place_t[...], sent).T
+            cols = slice(q * 128, (q + 1) * 128)
+            rows = dot(slot_hot[mode, pl.ds(q * 128, 128), :], source).T
+            for v in range(2):
+                first = max(left, v * FEAT_PAD)
+                last = min(left + width, v * FEAT_PAD + FEAT)
+                if first < last:
+                    fine[v, first - v * FEAT_PAD : last - v * FEAT_PAD, cols] = rows[first - left : last - left]
+
+    def store_start(v, step):
+        product = resid[v] + fine[v] * weight_ref[...]
+        fine[v] = product
+        stepped[v] = resid[v] - step[v : v + 1, 0:1] * product
+        copies = [
+            pltpu.make_async_copy(fine.at[v], product_hbm.at[:, v, :], load_sem.at[v]),
+            pltpu.make_async_copy(stepped.at[v], next_hbm.at[:, v, :], load_sem.at[3 + v]),
+        ]
+        for copy in copies:
+            copy.start()
+        return copies
+
+    arrived(out_0)
+    part_0 = part_start(0)
+    arrived(out_1)
+    part_1 = part_start(1)
     total[pl.ds(FEAT_PAD, FEAT_PAD), :] = jnp.zeros((FEAT_PAD, COARSE), F32)
+    arrived(part_0)
+    coarse_rows(0)
+    arrived(part_1)
+    coarse_rows(1)
     contract(0)
     sum_copies = sum_start(0)
+    arrived(out_2)
+    part_2 = part_start(2)
+    arrived(out_3)
+    part_3 = part_start(3)
     arrived(sum_copies)
     edge_copies = edges_start(0)
     arrived(edge_copies)
     share_copies = smooth_share(0)
 
-    arrived(out_copies_b)
-    coarse[pl.ds(OUT_CUT, WIDE - OUT_CUT), :] = dot(
-        place_t[...], recv_b[...].reshape(REGIONS * CAP, WIDE - OUT_CUT)
-    ).T
+    arrived(part_2)
+    coarse_rows(2)
+    arrived(part_3)
+    coarse_rows(3)
     contract(1)
     sum_copies_b = sum_start(1)
 
     arrived(share_copies)
     expand(0)
-    back_copies = back_start(0)
-
+    spread_0 = spread_start(0)
+    spread_1 = spread_start(1)
     arrived(sum_copies_b)
     edge_copies_b = edges_start(1)
+    arrived(spread_0)
+    back_0 = back_start(0)
+    arrived(spread_1)
+    back_1 = back_start(1)
     arrived(edge_copies_b)
     share_copies_b = smooth_share(1)
     norm_copies = []
@@ -416,7 +584,8 @@
         norm_copies.append(copy)
     arrived(share_copies_b)
     expand(1)
-    back_copies_b = back_start(1)
+    spread_2 = spread_start(2)
+    spread_3 = spread_start(3)
     arrived(norm_copies)
     norm_sum[...] = norm[...] + norm_in[0] + norm_in[1] + norm_in[2]
     last_copies = []
@@ -433,26 +602,34 @@
         last_copies.append(copy)
     norm_all[me] = norm_sum[...]
 
-    arrived(back_copies)
+    arrived(spread_2)
+    back_2 = back_start(2)
+    arrived(spread_3)
+    back_3 = back_start(3)
+
+    arrived(back_0)
     fine_rows(0)
+    arrived(back_1)
+    fine_rows(1)
     arrived(last_copies)
     sums = jnp.sum(jnp.sum(norm_all[...], axis=0), axis=1, keepdims=True)
     squares = jnp.broadcast_to(sums, (8, COARSE))
-    step_ref[...] = squares / (squares + pltpu.roll(squares, 6, 0))
-    arrived(back_copies_b)
-    fine_rows(1)
-    stores = [
-        pltpu.make_async_copy(fine.at[v], fine_hbm.at[:, v, :], load_sem.at[v])
-        for v in range(2)
-    ]
-    for copy in stores:
-        copy.start()
-    for copy in stores:
-        copy.wait()
-
+    step = squares / (squares + pltpu.roll(squares, 6, 0))
+    step_ref[...] = step
+    arrived(back_2)
+    fine_rows(2)
+    stores = store_start(0, step)
+    arrived(back_3)
+    fine_rows(3)
+    stores += store_start(1, step)
     for copies in (
-        out_copies,
-        out_copies_b,
+        index_copies,
+        out_2,
+        out_3,
+        part_0,
+        part_1,
+        part_2,
+        part_3,
         sum_copies,
         sum_copies_b,
         edge_copies,
@@ -461,18 +638,19 @@
         share_copies_b,
         norm_copies,
         last_copies,
-        back_copies,
-        back_copies_b,
+        spread_0,
+        spread_1,
+        spread_2,
+        spread_3,
+        back_0,
+        back_1,
+        back_2,
+        back_3,
     ):
         for copy in copies:
             copy.wait_send()
-
-
-def last_step(resid_ref, increment_ref, weight_ref, step_ref, product_ref, next_ref):
-    step = jnp.concatenate([step_ref[0:2, :]] * 4, axis=1)[None]
-    product = resid_ref[...] + increment_ref[...] * weight_ref[...][None]
-    product_ref[...] = product
-    next_ref[...] = resid_ref[...] - step * product
+    for copy in stores:
+        copy.wait()
 
 
 def per_device(residual, perturb, vertical_modes, column_weight, owner_table, column_map):
@@ -482,27 +660,30 @@
     whole = pl.BlockSpec(memory_space=pltpu.VMEM)
     anywhere = pl.BlockSpec(memory_space=pl.ANY)
     n = len(HOPS)
-    increment, step = pl.pallas_call(
+    product, next_residual, step = pl.pallas_call(
         kernel,
         out_shape=(
+            jax.ShapeDtypeStruct((FEAT, 2, FINE), F32),
             jax.ShapeDtypeStruct((FEAT, 2, FINE), F32),
             jax.ShapeDtypeStruct((8, COARSE), F32),
         ),
         in_specs=[whole] * 4 + [anywhere] * 2,
-        out_specs=(anywhere, whole),
+        out_specs=(anywhere, anywhere, whole),
         scratch_shapes=[
             vmem((2, FEAT, FINE), F32),
             vmem((FEAT_PAD, MEMBERS, COARSE), BF16),
             vmem((WIDE, FINE), F32),
             vmem((FINE, WIDE), BF16),
-            vmem((REGIONS * CAP, FINE), BF16),
-            vmem((FINE, REGIONS * CAP), BF16),
-            vmem((REGIONS * CAP, COARSE), BF16),
-            vmem((COARSE, REGIONS * CAP), BF16),
-            vmem((REGIONS, CAP, OUT_CUT), BF16),
-            vmem((REGIONS, CAP, WIDE - OUT_CUT), BF16),
-            vmem((REGIONS, CAP, OUT_CUT), BF16),
-            vmem((REGIONS, CAP, WIDE - OUT_CUT), BF16),
+            vmem((2, REGIONS * CAP, FINE), BF16),
+            vmem((2, FINE, REGIONS * CAP), BF16),
+            vmem((2, 8, 16, COARSE), BF16),
+            vmem((2, 8, 16, COARSE), BF16),
+            vmem((2, 4, 8 * CAP, COARSE), BF16),
+            vmem((2, 4, COARSE, 8 * CAP), BF16),
+            [vmem((8, 4, CAP, width), BF16) for _, width, _ in OUT],
+            [vmem((4, 8, CAP, width), BF16) for _, width, _ in OUT],
+            [vmem((4, COARSE, width), BF16) for _, width, _ in OUT],
+            [vmem((4, COARSE, width), BF16) for _, width, _ in OUT],
             vmem((WIDE, COARSE), F32),
             vmem((FEAT_PAD, 2 * SPREAD), F32),
             vmem((FEAT_PAD * GROUP, 2 * SPREAD), BF16),
@@ -516,21 +697,18 @@
             vmem((2, SHARE, COARSE), F32),
             vmem((2, SLOTS, SHARE, COARSE), BF16),
             vmem((WIDE, COARSE), F32),
-            vmem((COARSE, WIDE), BF16),
-            vmem((REGIONS, CAP, BACK_CUT), BF16),
-            vmem((REGIONS, CAP, WIDE - BACK_CUT), BF16),
-            vmem((REGIONS, CAP, BACK_CUT), BF16),
-            vmem((REGIONS, CAP, WIDE - BACK_CUT), BF16),
+            [vmem((COARSE, width), BF16) for _, width, _ in BACK],
+            [vmem((4, COARSE, width), BF16) for _, width, _ in BACK],
+            [vmem((8, 4, CAP, width), BF16) for _, width, _ in BACK],
+            [vmem((8, 4, CAP, width), BF16) for _, width, _ in BACK],
+            vmem((2, FEAT, FINE), F32),
             vmem((2, FEAT, FINE), F32),
             vmem((8, COARSE), F32),
             vmem((SLOTS - 1, 8, COARSE), F32),
             vmem((8, COARSE), F32),
             vmem((REGIONS, 8, COARSE), F32),
-            dma((3,)),
-            dma((2, n)),
-            dma((2, n)),
-            dma((2, n)),
-            dma((2, n)),
+            dma((5,)),
+            *[dma((rows, cols)) for rows, cols in ((2, 7), (4, 7), (4, 3), (4, 3), (4, 7)) for _ in range(2)],
             dma((2, 3)),
             dma((2, 3)),
             dma((2, 2)),
@@ -554,20 +732,6 @@
         resid_part,
         perturb[0].transpose(1, 0, 2),
     )
-    block = pl.BlockSpec((137, 2, FINE), lambda i: (i, 0, 0))
-    product, next_residual = pl.pallas_call(
-        last_step,
-        grid=(FEAT // 137,),
-        out_shape=(jax.ShapeDtypeStruct((FEAT, 2, FINE), F32),) * 2,
-        in_specs=[
-            block,
-            block,
-            pl.BlockSpec((1, FINE), lambda i: (0, 0)),
-            pl.BlockSpec((8, COARSE), lambda i: (0, 0)),
-        ],
-        out_specs=(block, block),
-        name="last_step",
-    )(resid_part, increment, weight, step)
     return (product.transpose(1, 0, 2)[None], step[0:2, 0], next_residual.transpose(1, 0, 2)[None])
 
 

time: 127 us -> 108 us (0.85)
  Pallas kernels: 124 us -> 99.9 us
  local copies, waits for them, and re-layouts: 1.3 us -> 7.32 us
    pallas_call x1, Pallas kernels: 117 us -> 99.9 us  [per_device(): pl.pallas_call(kernel, out_shape=(jax.ShapeDtypeStruct((FEAT, 2, FINE), F...]
    pallas_call x1 -> x0, Pallas kernels: 6.78 us -> none  [per_device(): pl.pallas_call(last_step, grid=(FEAT // 137,), out_shape=(jax.ShapeDtypeS...]
    unnamed x0 -> x4, local copies, waits for them, and re-layouts: none -> 6.01 us
where the time goes in v2:
time: 108 us
  Pallas kernels  99.9 us (92%)
  local copies, waits for them, and re-layouts  7.32 us (7%)
    pallas_call x1, Pallas kernels, per_device(): pl.pallas_call(kernel, out_shape=(jax.ShapeDtypeStruct((FEAT, 2, FINE), F...  99.9 us
    unnamed x4, local copies, waits for them, and re-layouts  6.01 us

profile of v2, /device:TPU:1, one launch (start us, length us, event | category | flops | bytes accessed | tf_op | source)
XLA Modules:
  0.0 107.9 jit_solution(4735008046824697901)
XLA Ops:
  0.6 99.9 %hessian.1 = (f32[685,2,512]{2,1,0:T(2,128)}, f32[685,2,512]{2,1,0:T(2,128)}, f32[8,128]{1,0:T(8,128)}) custom-call(s32[1,16384]{1,0:T(1,128)} %bitcast.20, s32[1,16384]{1,0:T(1,128)} %bitcast.21, f32[1,512]{1,0:T(1,128)} %bitcast.23, f32[10,685]{1,0:T(8,128)} %bitcast.22, f32[685,2,512]{2,1,0:T(2,128)} %bitcast.17, bf16[685,64,128]{2,1,0:T(8,128)(2,1)} %bitcast.16), custom_call_target="tpu_custom_call" | custom-call | tf_op jit(solution)/shard_map/hessian/pallas_call | solution.py:663
  100.6 1.3 %slice_reduce_fusion = f32[2]{0:T(128)} fusion(f32[8,128]{1,0:T(8,128)} %get-tuple-element.7), kind=kLoop, calls=%fused_computation | loop fusion | bytes 16 | tf_op jit(solution)/shard_map/slice | solution.py:735
  101.9 0.0 copy-start
  101.9 4.5 %copy.11 = f32[1,2,685,512]{3,1,2,0:T(2,128)} copy(f32[1,2,685,512]{3,1,2,0:T(2,128)} %bitcast.19) | data formatting | bytes 5611520
  106.3 0.0 copy-done
  106.3 1.6 %copy.12 = f32[1,2,685,512]{3,1,2,0:T(2,128)} copy(f32[1,2,685,512]{3,1,2,0:T(2,128)S(1)} %bitcast.18) | data formatting | bytes 5611520
Async XLA Ops:
  101.9 4.5 %copy-start = (f32[685,2,512]{2,1,0:T(2,128)S(1)}, f32[685,2,512]{2,1,0:T(2,128)}, u32[]{:S(2)}) copy-start(f32[685,2,512]{2,1,0:T(2,128)} %get-tuple-element.8) | copy-start | bytes 8417284

commit v3 on v2

--- a/solution.py
+++ b/solution.py
@@ -24,7 +24,7 @@
 ROWS = MODES * MEMBERS
 SHARE = ROWS // SLOTS
 OUT = ((0, 384, 0), (384, 384, 1), (768, 384, 0), (1152, 256, 1))
-BACK = ((0, 384, 0), (384, 256, 1), (640, 384, 0), (1024, 384, 1))
+BACK = ((0, 384, 0), (384, 256, 1), (640, 256, 0), (896, 256, 1), (1152, 128, 0), (1280, 128, 1))
 LINE = ((2, 0), (2, 1), (1, 0), (3, 0), (1, 1), (3, 1), (0, 1))
 GROUP = 8
 GROUPS = MEMBERS // GROUP
@@ -63,8 +63,7 @@
     modes_ref,
     resid_hbm,
     members_hbm,
-    product_hbm,
-    next_hbm,
+    fine_hbm,
     step_ref,
     resid,
     members,
@@ -98,7 +97,6 @@
     back,
     home,
     fine,
-    stepped,
     norm,
     norm_in,
     norm_sum,
@@ -171,14 +169,6 @@
     spare = FEAT_PAD - FEAT
     wide_rows[pl.ds(FEAT, spare), :] = jnp.zeros((spare, FINE), F32)
     wide_rows[pl.ds(FEAT_PAD + FEAT, spare), :] = jnp.zeros((spare, FINE), F32)
-    for v in range(2):
-        load_resid[v].wait()
-        wide_rows[pl.ds(v * FEAT_PAD, FEAT), :] = resid[v] * weight_ref[...]
-    load_members = pltpu.make_async_copy(members_hbm, members.at[pl.ds(0, FEAT)], load_sem.at[2])
-    load_members.start()
-    for q in range(4):
-        wide_cols[pl.ds(q * 128, 128), :] = wide_rows[:, q * 128 : (q + 1) * 128].T.astype(BF16)
-
     pl.semaphore_wait(barrier, len(HOPS) + 3)
 
     def spot(mode):
@@ -211,8 +201,15 @@
             b_to = (b + db) % 4
             yield j, b_to, {"region": device_at(mode, a, b_to, core)}
 
+    def weigh(v):
+        load_resid[v].wait()
+        wide_rows[pl.ds(v * FEAT_PAD, FEAT), :] = resid[v] * weight_ref[...]
+
     def pack(piece):
         left, width, mode = OUT[piece]
+        for q in range(4):
+            cols = slice(q * 128, (q + 1) * 128)
+            wide_cols[cols, left : left + width] = wide_rows[left : left + width, cols].T.astype(BF16)
 
         def one(q, carry):
             rows = slot_hot_t[mode, pl.ds(pl.multiple_of(q * 256, 256), 256), :]
@@ -281,8 +278,12 @@
                 )
             )
         index_in[mode, here] = index_out[mode, here]
+    weigh(0)
     pack(0)
     out_0 = out_start(0, None)
+    weigh(1)
+    load_members = pltpu.make_async_copy(members_hbm, members.at[pl.ds(0, FEAT)], load_sem.at[2])
+    load_members.start()
     pack(1)
     out_1 = out_start(1, None)
     pack(2)
@@ -336,8 +337,6 @@
             hot = hot.astype(F32)
             place_t[mode, b] = hot.astype(BF16)
             place[mode, b] = hot.T.astype(BF16)
-    out_2 = out_start(2, out_0)
-    out_3 = out_start(3, out_1)
     load_members.wait()
 
     def contract(v):
@@ -519,14 +518,8 @@
                 if first < last:
                     fine[v, first - v * FEAT_PAD : last - v * FEAT_PAD, cols] = rows[first - left : last - left]
 
-    def store_start(v, step):
-        product = resid[v] + fine[v] * weight_ref[...]
-        fine[v] = product
-        stepped[v] = resid[v] - step[v : v + 1, 0:1] * product
-        copies = [
-            pltpu.make_async_copy(fine.at[v], product_hbm.at[:, v, :], load_sem.at[v]),
-            pltpu.make_async_copy(stepped.at[v], next_hbm.at[:, v, :], load_sem.at[3 + v]),
-        ]
+    def store_start(v):
+        copies = [pltpu.make_async_copy(fine.at[v], fine_hbm.at[:, v, :], load_sem.at[v])]
         for copy in copies:
             copy.start()
         return copies
@@ -535,6 +528,8 @@
     part_0 = part_start(0)
     arrived(out_1)
     part_1 = part_start(1)
+    out_2 = out_start(2, out_0)
+    out_3 = out_start(3, out_1)
     total[pl.ds(FEAT_PAD, FEAT_PAD), :] = jnp.zeros((FEAT_PAD, COARSE), F32)
     arrived(part_0)
     coarse_rows(0)
@@ -564,12 +559,12 @@
     spread_1 = spread_start(1)
     arrived(sum_copies_b)
     edge_copies_b = edges_start(1)
+    arrived(edge_copies_b)
+    share_copies_b = smooth_share(1)
     arrived(spread_0)
     back_0 = back_start(0)
     arrived(spread_1)
     back_1 = back_start(1)
-    arrived(edge_copies_b)
-    share_copies_b = smooth_share(1)
     norm_copies = []
     for d in (2, 1, 3):
         copy = pltpu.make_async_remote_copy(
@@ -586,6 +581,8 @@
     expand(1)
     spread_2 = spread_start(2)
     spread_3 = spread_start(3)
+    spread_4 = spread_start(4)
+    spread_5 = spread_start(5)
     arrived(norm_copies)
     norm_sum[...] = norm[...] + norm_in[0] + norm_in[1] + norm_in[2]
     last_copies = []
@@ -606,6 +603,10 @@
     back_2 = back_start(2)
     arrived(spread_3)
     back_3 = back_start(3)
+    arrived(spread_4)
+    back_4 = back_start(4)
+    arrived(spread_5)
+    back_5 = back_start(5)
 
     arrived(back_0)
     fine_rows(0)
@@ -618,10 +619,14 @@
     step_ref[...] = step
     arrived(back_2)
     fine_rows(2)
-    stores = store_start(0, step)
+    stores = store_start(0)
     arrived(back_3)
     fine_rows(3)
-    stores += store_start(1, step)
+    arrived(back_4)
+    fine_rows(4)
+    arrived(back_5)
+    fine_rows(5)
+    stores += store_start(1)
     for copies in (
         index_copies,
         out_2,
@@ -642,10 +647,14 @@
         spread_1,
         spread_2,
         spread_3,
+        spread_4,
+        spread_5,
         back_0,
         back_1,
         back_2,
         back_3,
+        back_4,
+        back_5,
     ):
         for copy in copies:
             copy.wait_send()
@@ -660,15 +669,14 @@
     whole = pl.BlockSpec(memory_space=pltpu.VMEM)
     anywhere = pl.BlockSpec(memory_space=pl.ANY)
     n = len(HOPS)
-    product, next_residual, step = pl.pallas_call(
+    increment, step = pl.pallas_call(
         kernel,
         out_shape=(
-            jax.ShapeDtypeStruct((FEAT, 2, FINE), F32),
             jax.ShapeDtypeStruct((FEAT, 2, FINE), F32),
             jax.ShapeDtypeStruct((8, COARSE), F32),
         ),
         in_specs=[whole] * 4 + [anywhere] * 2,
-        out_specs=(anywhere, anywhere, whole),
+        out_specs=(anywhere, whole),
         scratch_shapes=[
             vmem((2, FEAT, FINE), F32),
             vmem((FEAT_PAD, MEMBERS, COARSE), BF16),
@@ -702,13 +710,12 @@
             [vmem((8, 4, CAP, width), BF16) for _, width, _ in BACK],
             [vmem((8, 4, CAP, width), BF16) for _, width, _ in BACK],
             vmem((2, FEAT, FINE), F32),
-            vmem((2, FEAT, FINE), F32),
             vmem((8, COARSE), F32),
             vmem((SLOTS - 1, 8, COARSE), F32),
             vmem((8, COARSE), F32),
             vmem((REGIONS, 8, COARSE), F32),
-            dma((5,)),
-            *[dma((rows, cols)) for rows, cols in ((2, 7), (4, 7), (4, 3), (4, 3), (4, 7)) for _ in range(2)],
+            dma((3,)),
+            *[dma((rows, cols)) for rows, cols in ((2, 7), (4, 7), (4, 3), (6, 3), (6, 7)) for _ in range(2)],
             dma((2, 3)),
             dma((2, 3)),
             dma((2, 2)),
@@ -732,7 +739,10 @@
         resid_part,
         perturb[0].transpose(1, 0, 2),
     )
-    return (product.transpose(1, 0, 2)[None], step[0:2, 0], next_residual.transpose(1, 0, 2)[None])
+    step_length = step[0:2, 0]
+    product = resid_part + increment * column_weight[None, None, :]
+    next_residual = resid_part - step_length[None, :, None] * product
+    return (product.transpose(1, 0, 2)[None], step_length, next_residual.transpose(1, 0, 2)[None])
 
 
 def solution(mesh):

time: 108 us -> 102 us (0.944)
  local copies, waits for them, and re-layouts: 7.32 us -> 0.81 us
  other arithmetic: 0 us -> 6.27 us
  Pallas kernels: 99.9 us -> 94.3 us
    broadcast_in_dim x0 -> x1, other arithmetic: none -> 6.27 us  [per_device(): next_residual.transpose(1, 0, 2)[None]]
    unnamed x4 -> x6, local copies, waits for them, and re-layouts: 6.01 us -> 0.02 us
    pallas_call x1, Pallas kernels: 99.9 us -> 94.3 us  [per_device(): pl.pallas_call(kernel, out_shape=(jax.ShapeDtypeStruct((FEAT, 2, FINE), F...]
where the time goes in v3:
time: 102 us
  Pallas kernels  94.3 us (92%)
  other arithmetic  6.27 us (6%)
    pallas_call x1, Pallas kernels, per_device(): pl.pallas_call(kernel, out_shape=(jax.ShapeDtypeStruct((FEAT, 2, FINE), F...  94.3 us
    broadcast_in_dim x1, other arithmetic, per_device(): next_residual.transpose(1, 0, 2)[None]  6.27 us

profile of v3, /device:TPU:1, one launch (start us, length us, event | category | flops | bytes accessed | tf_op | source)
XLA Modules:
  0.0 102.1 jit_solution(10895862703844352015)
XLA Ops:
  0.6 0.0 copy-start
  0.6 0.0 copy-start.1
  0.7 94.3 %hessian.1 = (f32[685,2,512]{2,1,0:T(2,128)}, f32[8,128]{1,0:T(8,128)}) custom-call(s32[1,16384]{1,0:T(1,128)} %bitcast.22, s32[1,16384]{1,0:T(1,128)} %bitcast.23, f32[1,512]{1,0:T(1,128)} %bitcast.25, f32[10,685]{1,0:T(8,128)} %bitcast.24, f32[685,2,512]{2,1,0:T(2,128)} %bitcast.21, bf16[685,64,128]{2,1,0:T(8,128)(2,1)} %bitcast.20), custom_call_target="tpu_custom_call" | custom-call | tf_op jit(solution)/shard_map/hessian/pallas_call | solution.py:672
  95.0 0.8 slice_reduce_fusion
  95.8 0.0 copy-done
  95.8 0.0 copy-done.1
  95.8 0.0 copy-start.2
  95.8 6.3 %subtract_bitcast_fusion = (f32[1,2,685,512]{3,1,2,0:T(2,128)}, f32[1,2,685,512]{3,1,2,0:T(2,128)}) fusion(f32[685,2,512]{2,1,0:T(2,128)} %get-tuple-element.5, f32[2]{0:T(128)S(1)} %slice_reduce_fusion, f32[512]{0:T(512)S(1)} %copy-done.1, f32[1,2,685,512]{3,1,2,0:T(2,128)S(1)} %copy-done), kind=kLoop, calls=%fused_computation | loop fusion | flops 2805760 | bytes 11225096 | tf_op jit(solution)/shard_map/broadcast_in_dim | solution.py:745
  102.1 0.0 copy-done.2
Async XLA Ops:
  0.6 95.2 %copy-start = (f32[1,2,685,512]{3,1,2,0:T(2,128)S(1)}, f32[1,2,685,512]{3,1,2,0:T(2,128)}, u32[]{:S(2)}) copy-start(f32[1,2,685,512]{3,1,2,0:T(2,128)} %param.6) | copy-start | bytes 8417284
  0.6 95.2 %copy-start.1 = (f32[512]{0:T(512)S(1)}, f32[512]{0:T(512)}, u32[]{:S(2)}) copy-start(f32[512]{0:T(512)} %param.9) | copy-start | bytes 6148
  95.8 6.3 %copy-start.2 = (f32[2]{0:T(128)}, f32[2]{0:T(128)S(1)}, u32[]{:S(2)}) copy-start(f32[2]{0:T(128)S(1)} %slice_reduce_fusion) | copy-start | bytes 28

commit v4 on v3

--- a/solution.py
+++ b/solution.py
@@ -660,6 +660,29 @@
             copy.wait_send()
     for copy in stores:
         copy.wait()
+
+
+def last_step(resid_ref, increment_ref, weight_ref, step_ref, product_ref, next_ref, length_ref):
+    cut = (resid_ref.shape[0] // 8, 8, COARSE)
+    row = lax.broadcasted_iota(jnp.int32, (8, COARSE), 0)
+    step = jnp.where(row % 2 == 1, step_ref[1:2, :], step_ref[0:1, :])
+    weight = weight_ref[:, 0:COARSE]
+    for j in range(1, 4):
+        weight = jnp.where(row // 2 == j, weight_ref[:, j * COARSE : (j + 1) * COARSE], weight)
+    for v in range(2):
+        length_ref[v] = jnp.max(step_ref[v : v + 1, :])
+    resid = resid_ref[...].reshape(cut)
+    product = resid + increment_ref[...].reshape(cut) * weight[None]
+    product_ref[...] = product.reshape(resid_ref.shape)
+    next_ref[...] = (resid - step[None] * product).reshape(resid_ref.shape)
+
+
+def by_lanes(fields):
+    return fields.reshape(FEAT, 2, 4, COARSE).transpose(0, 2, 1, 3).reshape(FEAT * 8, COARSE)
+
+
+def by_fields(rows):
+    return rows.reshape(FEAT, 4, 2, COARSE).transpose(2, 0, 1, 3).reshape(1, 2, FEAT, FINE)
 
 
 def per_device(residual, perturb, vertical_modes, column_weight, owner_table, column_map):
@@ -739,10 +762,23 @@
         resid_part,
         perturb[0].transpose(1, 0, 2),
     )
-    step_length = step[0:2, 0]
-    product = resid_part + increment * column_weight[None, None, :]
-    next_residual = resid_part - step_length[None, :, None] * product
-    return (product.transpose(1, 0, 2)[None], step_length, next_residual.transpose(1, 0, 2)[None])
+    rows = FEAT // 5 * 8
+    block = pl.BlockSpec((rows, COARSE), lambda i: (i, 0))
+    small = pl.BlockSpec((8, COARSE), lambda i: (0, 0))
+    product, next_residual, step_length = pl.pallas_call(
+        last_step,
+        grid=(5,),
+        out_shape=(jax.ShapeDtypeStruct((FEAT * 8, COARSE), F32),) * 2 + (jax.ShapeDtypeStruct((2,), F32),),
+        in_specs=[block, block, pl.BlockSpec((1, FINE), lambda i: (0, 0)), small],
+        out_specs=(block, block, pl.BlockSpec(memory_space=pltpu.SMEM)),
+        name="last_step",
+    )(
+        by_lanes(resid_part),
+        by_lanes(increment),
+        weight,
+        step,
+    )
+    return (by_fields(product), step_length, by_fields(next_residual))
 
 
 def solution(mesh):

time: 102 us -> 101 us (level)
  other arithmetic: 6.27 us -> 0 us
  Pallas kernels: 94.3 us -> 100 us
    pallas_call x0 -> x1, Pallas kernels: none -> 6.86 us  [per_device(): pl.pallas_call(last_step, grid=(5,), out_shape=(jax.ShapeDtypeStruct((FEA...]
    broadcast_in_dim x1 -> x0, other arithmetic: 6.27 us -> none  [per_device(): next_residual.transpose(1, 0, 2)[None]]
where the time goes in v4:
time: 101 us
  Pallas kernels  100 us (99%)
    pallas_call x1, Pallas kernels, per_device(): pl.pallas_call(kernel, out_shape=(jax.ShapeDtypeStruct((FEAT, 2, FINE), F...  93.6 us
    pallas_call x1, Pallas kernels, per_device(): pl.pallas_call(last_step, grid=(5,), out_shape=(jax.ShapeDtypeStruct((FEA...  6.86 us

profile of v4, /device:TPU:1, one launch (start us, length us, event | category | flops | bytes accessed | tf_op | source)
XLA Modules:
  0.0 101.1 jit_solution(12434164035992366048)
XLA Ops:
  0.6 93.6 %hessian.1 = (f32[685,2,512]{2,1,0:T(2,128)}, f32[8,128]{1,0:T(8,128)}) custom-call(s32[1,16384]{1,0:T(1,128)} %bitcast.35, s32[1,16384]{1,0:T(1,128)} %bitcast.36, f32[1,512]{1,0:T(1,128)} %bitcast.38, f32[10,685]{1,0:T(8,128)} %bitcast.37, f32[685,2,512]{2,1,0:T(2,128)} %bitcast.32, bf16[685,64,128]{2,1,0:T(8,128)(2,1)} %bitcast.31), custom_call_target="tpu_custom_call" | custom-call | tf_op jit(solution)/shard_map/hessian/pallas_call | solution.py:695
  94.2 6.9 %last_step.1 = (f32[5480,128]{1,0:T(8,128)}, f32[5480,128]{1,0:T(8,128)}, f32[2]{0:T(128)}) custom-call(f32[5480,128]{1,0:T(8,128)} %bitcast.33, f32[5480,128]{1,0:T(8,128)} %bitcast.34, f32[1,512]{1,0:T(1,128)} %bitcast.39, f32[8,128]{1,0:T(8,128)} %get-tuple-element.9.step_ref), custom_call_target="tpu_custom_call" | custom-call | tf_op jit(solution)/shard_map/last_step/pallas_call | solution.py:768

commit v5 on v4

--- a/solution.py
+++ b/solution.py
@@ -30,6 +30,7 @@
 GROUPS = MEMBERS // GROUP
 SPREAD = MODES * GROUP
 STEP = 176
+WIDE_STEP = 352
 
 NEAR_FIRST = (
     [(0, 1), (1, 0), (0, 3), (3, 0)],
@@ -452,19 +453,19 @@
             mode_cells[SPREAD:, g * COARSE : (g + 1) * COARSE] = cells
 
         def chunk(i, carry):
-            left = mixer[pl.ds(pl.multiple_of(i * STEP * GROUP, STEP * GROUP), STEP * GROUP), :]
-            cells = members[pl.ds(i * STEP, STEP)].astype(F32).reshape(STEP, GROUPS, GROUP, COARSE)
-            sums = jnp.zeros((STEP, GROUP, COARSE), F32)
+            left = mixer[pl.ds(pl.multiple_of(i * WIDE_STEP * GROUP, WIDE_STEP * GROUP), WIDE_STEP * GROUP), :]
+            cells = members[pl.ds(i * WIDE_STEP, WIDE_STEP)].astype(F32).reshape(WIDE_STEP, GROUPS, GROUP, COARSE)
+            sums = jnp.zeros((WIDE_STEP, GROUP, COARSE), F32)
             for pair in range(GROUPS // 2):
                 mixed = dot(left, mode_cells[:, pair * 256 : (pair + 1) * 256])
                 for e in range(2):
-                    part = mixed[:, e * COARSE : (e + 1) * COARSE].reshape(STEP, GROUP, COARSE)
+                    part = mixed[:, e * COARSE : (e + 1) * COARSE].reshape(WIDE_STEP, GROUP, COARSE)
                     sums = sums + cells[:, 2 * pair + e] * part
-            at = pl.ds(pl.multiple_of(v * FEAT_PAD + i * STEP, STEP), STEP)
+            at = pl.ds(pl.multiple_of(v * FEAT_PAD + i * WIDE_STEP, WIDE_STEP), WIDE_STEP)
             total[at, :] = jnp.sum(sums, axis=1)
             return carry
 
-        lax.fori_loop(0, FEAT_PAD // STEP, chunk, 0)
+        lax.fori_loop(0, FEAT_PAD // WIDE_STEP, chunk, 0)
 
     def arrived(copies):
         for copy in copies:

time: 101 us -> 101 us (level)
  no operation moved by 1% of the time
where the time goes in v5:
time: 101 us
  Pallas kernels  100 us (99%)
    pallas_call x1, Pallas kernels, per_device(): pl.pallas_call(kernel, out_shape=(jax.ShapeDtypeStruct((FEAT, 2, FINE), F...  93.3 us
    pallas_call x1, Pallas kernels, per_device(): pl.pallas_call(last_step, grid=(5,), out_shape=(jax.ShapeDtypeStruct((FEA...  6.86 us

profile of v5, /device:TPU:1, one launch (start us, length us, event | category | flops | bytes accessed | tf_op | source)
XLA Modules:
  0.0 100.8 jit_solution(14330664700689453010)
XLA Ops:
  0.6 93.3 %hessian.1 = (f32[685,2,512]{2,1,0:T(2,128)}, f32[8,128]{1,0:T(8,128)}) custom-call(s32[1,16384]{1,0:T(1,128)} %bitcast.35, s32[1,16384]{1,0:T(1,128)} %bitcast.36, f32[1,512]{1,0:T(1,128)} %bitcast.38, f32[10,685]{1,0:T(8,128)} %bitcast.37, f32[685,2,512]{2,1,0:T(2,128)} %bitcast.32, bf16[685,64,128]{2,1,0:T(8,128)(2,1)} %bitcast.31), custom_call_target="tpu_custom_call" | custom-call | tf_op jit(solution)/shard_map/hessian/pallas_call | solution.py:696
  93.9 6.9 %last_step.1 = (f32[5480,128]{1,0:T(8,128)}, f32[5480,128]{1,0:T(8,128)}, f32[2]{0:T(128)}) custom-call(f32[5480,128]{1,0:T(8,128)} %bitcast.33, f32[5480,128]{1,0:T(8,128)} %bitcast.34, f32[1,512]{1,0:T(1,128)} %bitcast.39, f32[8,128]{1,0:T(8,128)} %get-tuple-element.9.step_ref), custom_call_target="tpu_custom_call" | custom-call | tf_op jit(solution)/shard_map/last_step/pallas_call | solution.py:769
